TPU v7x, 128 devices: a whole 4x4x4 slice. The times are simulated.
128 devices in a mesh: ctx: 32 (over z, x_lo, y), tp: 4 (over x_hi, core).
Axes of the slice: x: 4 (x_hi: 2, x_lo: 2; x = x_hi * 2 + x_lo), y: 4, z: 4, core: 2. Of those that a mesh axis runs over, the one named last changes fastest.
Arguments:
- q_self: bfloat16 [6144, 2560], P('ctx', 'tp'), may hold values from -64 to 64
- k_self: bfloat16 [6144, 2560], P('ctx', 'tp'), may hold values from -64 to 64
- v_self: bfloat16 [6144, 2560], P('ctx', 'tp'), may hold values from -6 to 6
- grad_self: bfloat16 [6144, 2560], P('ctx', 'tp'), may hold values from -448 to 448
- q_cross: bfloat16 [6144, 2560], P('ctx', 'tp'), may hold values from -64 to 64
- grad_cross: bfloat16 [6144, 2560], P('ctx', 'tp'), may hold values from -80 to 80
- k_text: bfloat16 [512, 2560], P(None, 'tp'), may hold values from -64 to 64
- v_text: bfloat16 [512, 2560], P(None, 'tp'), may hold values from -6 to 6
- gain_q: float32 [2560], P('tp'), may hold values from 0.1 to 1.9
- gain_k: float32 [2560], P('tp'), may hold values from 0.1 to 1.9
- gain_cross_q: float32 [2560], P('tp'), may hold values from 0.1 to 1.9
- gain_text_k: float32 [2560], P('tp'), may hold values from 0.1 to 1.9
Outputs:
- grad_q_self: bfloat16 [6144, 2560], P('ctx', 'tp')
- grad_k_self: bfloat16 [6144, 2560], P('ctx', 'tp')
- grad_v_self: bfloat16 [6144, 2560], P('ctx', 'tp')
- grad_q_cross: bfloat16 [6144, 2560], P('ctx', 'tp')
- grad_k_text: bfloat16 [512, 2560], P(None, 'tp')
- grad_v_text: bfloat16 [512, 2560], P(None, 'tp')
All inputs are finite; a program needn't handle non-finite values.
Results may differ from a plain program's by a relative error of at most 0.034.
Values may be sent and summed in bfloat16 or wider, within the bound.
No kernel may reach another device: no remote copies, remote signals or barrier semaphores. Data moves between devices by JAX's collectives and lax.ppermute only.
A program may use at most 192 MiB of HBM per device.

v0:
```python
import jax
import jax.numpy as jnp
from jax import lax
from jax.sharding import PartitionSpec as P

HD = 128
epsilon = 1e-06


def squares(tensor):
    floats = tensor.astype(jnp.float32)
    return jnp.sum(floats * floats, axis=1)


def normalize(tensor, square_sum, gain, features):
    inverse = lax.rsqrt(square_sum / features + epsilon)[:, None]
    return ((tensor.astype(jnp.float32) * inverse * gain).astype(jnp.bfloat16), inverse)


def by_heads(tensor):
    return tensor.reshape(tensor.shape[0], -1, HD)


def into_blocks(tensor, span):
    return tensor.reshape(tensor.shape[0] // span, span, -1, HD)


def start_state(query_heads):
    row_count = query_heads.shape[0]
    head_count = query_heads.shape[1]
    return (
        jnp.full((head_count, row_count), -1e30, jnp.float32),
        jnp.zeros((head_count, row_count), jnp.float32),
        jnp.zeros((head_count, row_count), jnp.float32),
    )


def forward_step(running, query_heads, grad_heads, key_heads, value_heads):
    maximum, totals, weighted = running
    scores = jnp.einsum(
        "qhd,khd->hqk", query_heads, key_heads, preferred_element_type=jnp.float32
    ) * HD ** (-0.5)
    grad_prob = jnp.einsum(
        "qhd,khd->hqk", grad_heads, value_heads, preferred_element_type=jnp.float32
    )
    new_max = jnp.maximum(maximum, jnp.max(scores, axis=2))
    factor = jnp.exp(maximum - new_max)
    weights = jnp.exp(scores - new_max[:, :, None])
    totals = totals * factor + jnp.sum(weights, axis=2)
    weighted = weighted * factor + jnp.sum(weights * grad_prob, axis=2)
    return (new_max, totals, weighted)


def finish(running):
    maximum, totals, weighted = running
    return (maximum + jnp.log(totals), weighted / totals)


def backward_terms(query_heads, grad_heads, logsum, deltas, key_heads, value_heads):
    scaling = HD ** (-0.5)
    scores = (
        jnp.einsum("qhd,khd->hqk", query_heads, key_heads, preferred_element_type=jnp.float32)
        * scaling
    )
    probability = jnp.exp(scores - logsum[:, :, None])
    grad_prob = jnp.einsum(
        "qhd,khd->hqk", grad_heads, value_heads, preferred_element_type=jnp.float32
    )
    grad_score = (probability * (grad_prob - deltas[:, :, None])).astype(jnp.bfloat16)
    results = []
    results.append(
        jnp.einsum("hqk,khd->qhd", grad_score, key_heads, preferred_element_type=jnp.float32)
        * scaling
    )
    results.append(
        jnp.einsum("hqk,qhd->khd", grad_score, query_heads, preferred_element_type=jnp.float32)
        * scaling
    )
    results.append(
        jnp.einsum(
            "hqk,qhd->khd",
            probability.astype(jnp.bfloat16),
            grad_heads,
            preferred_element_type=jnp.float32,
        )
    )
    return results


def forward_pass(query_heads, grad_heads, key_blocks, value_blocks):

    def forward_advance(running, blocks):
        return (forward_step(running, query_heads, grad_heads, blocks[0], blocks[1]), None)

    return lax.scan(forward_advance, start_state(query_heads), (key_blocks, value_blocks))[0]


def query_pass(query_heads, grad_heads, logsum, deltas, key_blocks, value_blocks):

    def query_advance(grad_query, blocks):
        terms = backward_terms(query_heads, grad_heads, logsum, deltas, blocks[0], blocks[1])
        return (grad_query + terms[0], tuple(terms[1:]))

    return lax.scan(
        query_advance, jnp.zeros(query_heads.shape, jnp.float32), (key_blocks, value_blocks)
    )


def norm_terms(tensor, inverse, gain, gradient):
    unit_rows = tensor.astype(jnp.float32) * inverse
    scaled = gradient * gain
    return (unit_rows, scaled, jnp.sum(scaled * unit_rows, axis=1))


def norm_result(inverse, terms, summed, features):
    return (inverse * (terms[1] - terms[0] * (summed / features)[:, None])).astype(jnp.bfloat16)


def local(
    q_self,
    k_self,
    v_self,
    grad_self,
    q_cross,
    grad_cross,
    k_text,
    v_text,
    gain_q,
    gain_k,
    gain_cross_q,
    gain_text_k,
):
    features = q_self.shape[1] * lax.axis_size("tp")
    row_count = q_self.shape[0]
    text_rows = k_text.shape[0]
    span = 4 * row_count
    sums = lax.psum((squares(q_self), squares(k_self), squares(q_cross), squares(k_text)), "tp")
    query_norm, inverse_q = normalize(q_self, sums[0], gain_q, features)
    key_norm, inverse_k = normalize(k_self, sums[1], gain_k, features)
    cross_norm, inverse_c = normalize(q_cross, sums[2], gain_cross_q, features)
    text_norm, inverse_t = normalize(k_text, sums[3], gain_text_k, features)
    query_heads = by_heads(query_norm)
    grad_heads = by_heads(grad_self)
    key_all, value_all = (
        lax.all_gather(key_norm, "ctx", axis=0, tiled=True),
        lax.all_gather(v_self, "ctx", axis=0, tiled=True),
    )
    key_blocks = into_blocks(key_all, span)
    value_blocks = into_blocks(value_all, span)
    logsum, deltas = finish(forward_pass(query_heads, grad_heads, key_blocks, value_blocks))
    grad_query, stacked = query_pass(
        query_heads, grad_heads, logsum, deltas, key_blocks, value_blocks
    )
    grad_key, grad_value = (
        lax.psum_scatter(
            stacked[0].reshape(key_all.shape).astype(jnp.bfloat16),
            "ctx",
            scatter_dimension=0,
            tiled=True,
        ).astype(jnp.float32),
        lax.psum_scatter(
            stacked[1].reshape(key_all.shape).astype(jnp.bfloat16),
            "ctx",
            scatter_dimension=0,
            tiled=True,
        ).astype(jnp.float32),
    )
    cross_heads = by_heads(cross_norm)
    cross_grads = by_heads(grad_cross)
    text_heads = by_heads(text_norm)
    text_values = by_heads(v_text)
    cross_state = forward_step(
        start_state(cross_heads), cross_heads, cross_grads, text_heads, text_values
    )
    cross_logsum, cross_deltas = finish(cross_state)
    cross_terms = backward_terms(
        cross_heads, cross_grads, cross_logsum, cross_deltas, text_heads, text_values
    )
    text_key_grad, text_value_grad = (
        lax.psum(cross_terms[1].reshape(text_rows, -1).astype(jnp.bfloat16), "ctx").astype(
            jnp.float32
        ),
        lax.psum(cross_terms[2].reshape(text_rows, -1).astype(jnp.bfloat16), "ctx").astype(
            jnp.float32
        ),
    )
    pieces_q = norm_terms(q_self, inverse_q, gain_q, grad_query.reshape(row_count, -1))
    pieces_k = norm_terms(k_self, inverse_k, gain_k, grad_key.reshape(row_count, -1))
    pieces_c = norm_terms(q_cross, inverse_c, gain_cross_q, cross_terms[0].reshape(row_count, -1))
    pieces_t = norm_terms(k_text, inverse_t, gain_text_k, text_key_grad)
    row_sums = lax.psum((pieces_q[2], pieces_k[2], pieces_c[2], pieces_t[2]), "tp")
    return (
        norm_result(inverse_q, pieces_q, row_sums[0], features),
        norm_result(inverse_k, pieces_k, row_sums[1], features),
        grad_value.reshape(row_count, -1).astype(jnp.bfloat16),
        norm_result(inverse_c, pieces_c, row_sums[2], features),
        norm_result(inverse_t, pieces_t, row_sums[3], features),
        text_value_grad.astype(jnp.bfloat16),
    )


def solution(mesh):
    in_specs = (
        P("ctx", "tp"),
        P("ctx", "tp"),
        P("ctx", "tp"),
        P("ctx", "tp"),
        P("ctx", "tp"),
        P("ctx", "tp"),
        P(None, "tp"),
        P(None, "tp"),
        P("tp"),
        P("tp"),
        P("tp"),
        P("tp"),
    )
    out_specs = (
        P("ctx", "tp"),
        P("ctx", "tp"),
        P("ctx", "tp"),
        P("ctx", "tp"),
        P(None, "tp"),
        P(None, "tp"),
    )
    return jax.shard_map(local, mesh=mesh, in_specs=in_specs, out_specs=out_specs, check_vma=False)
```

profile of v0, /device:TPU:4, one launch (start us, length us, event | category | flops | bytes accessed | tf_op | source)
XLA Modules:
  0.0 1038.5 jit_solution(16445170293063702059)
XLA Ops:
  12.7 7.4 all-reduce.1
  24.9 2.1 fusion.29
  28.4 2.2 copy.95
  30.6 2.0 multiply_convert_fusion.1
  35.8 154.5 %all-gather.3.cloned.1.call-done = bf16[6144,640]{1,0:T(8,128)(2,1)} async-done(((bf16[192,640]{1,0:T(8,128)(2,1)}), bf16[6144,640]{1,0:T(8,128)(2,1)}) %all-gather.3.cloned.1.call-update) | async-done | bytes 7864336 | tf_op jit(solution)/shard_map/all_gather | solution.py:145
  190.3 18.1 %reshape.100 = bf16[8,768,5,128]{3,2,1,0:T(8,128)(2,1)} reshape(bf16[6144,640]{1,0:T(8,128)(2,1)} %all-gather.3.cloned.1.call-done) | data formatting | bytes 15728640 | tf_op jit(solution)/shard_map/reshape | solution.py:25
  208.4 9.9 copy.75
  218.4 140.3 %all-gather.5.cloned.1.call-done = bf16[6144,640]{1,0:T(8,128)(2,1)} async-done(((bf16[192,640]{1,0:T(8,128)(2,1)}), bf16[6144,640]{1,0:T(8,128)(2,1)}) %all-gather.5.cloned.1.call-update) | async-done | bytes 7864336 | tf_op jit(solution)/shard_map/all_gather | solution.py:146
  358.6 18.1 %reshape.101 = bf16[8,768,5,128]{3,2,1,0:T(8,128)(2,1)} reshape(bf16[6144,640]{1,0:T(8,128)(2,1)} %all-gather.5.cloned.1.call-done) | data formatting | bytes 15728640 | tf_op jit(solution)/shard_map/reshape | solution.py:25
  376.7 10.0 copy.73
  386.7 38.2 %while.30 = (s32[]{:T(128)}, f32[5,192]{1,0:T(8,128)S(1)}, f32[5,192]{1,0:T(8,128)S(1)}, f32[5,192]{1,0:T(8,128)S(1)}, bf16[8,768,5,128]{3,1,2,0:T(8,128)(2,1)},...) while((s32[]{:T(128)}, f32[5,192]{1,0:T(8,128)S(1)}, ...), condition=%wide.region_8.9_spmd.clone, body=%wide.region_4.8_spmd.clone.sunk | while | flops 384129600 | bytes 11374208 | solution.py:95
  386.7 1.8 bitcast_reduce_fusion.2
  388.6 2.1 fusion.112
  391.5 1.8 bitcast_reduce_fusion.2
  393.4 2.1 fusion.112
  396.3 1.8 bitcast_reduce_fusion.2
  398.2 2.1 fusion.112
  401.1 1.8 bitcast_reduce_fusion.2
  402.9 2.1 fusion.112
  405.9 1.8 bitcast_reduce_fusion.2
  407.7 2.1 fusion.112
  410.6 1.8 bitcast_reduce_fusion.2
  412.5 2.1 fusion.112
  415.4 1.8 bitcast_reduce_fusion.2
  417.3 2.1 fusion.112
  420.2 1.8 bitcast_reduce_fusion.2
  422.0 2.1 fusion.112
  425.0 96.3 %while.31 = (s32[]{:T(128)}, f32[192,5,128]{2,0,1:T(8,128)}, bf16[8,768,5,128]{3,1,2,0:T(8,128)(2,1)}, bf16[8,768,5,128]{3,1,2,0:T(8,128)(2,1)}, bf16[8,768,5,12...) while((s32[]{:T(128)}, f32[192,5,128]{2,0,1:T(8,128)}, ...), condition=%wide.region_10.0_spmd.clone, body=%wide.region_9.0_spmd.clone.sunk | while | flops 950476800 | bytes 28028344 | solution.py:104
  426.7 3.2 multiply_convert_fusion.3
  429.9 3.1 fusion.126
  434.8 2.1 bitcast_dynamic-update-slice_fusion.5
  438.7 3.2 multiply_convert_fusion.3
  441.8 3.2 fusion.126
  445.0 1.9 bitcast_dynamic-update-slice_fusion.4
  446.9 2.1 bitcast_dynamic-update-slice_fusion.5
  450.8 3.2 multiply_convert_fusion.3
  453.9 3.2 fusion.126
  459.0 2.1 bitcast_dynamic-update-slice_fusion.5
  462.8 3.2 multiply_convert_fusion.3
  466.0 3.2 fusion.126
  471.0 2.1 bitcast_dynamic-update-slice_fusion.5
  474.8 3.2 multiply_convert_fusion.3
  478.0 3.2 fusion.126
  481.2 1.8 bitcast_dynamic-update-slice_fusion.4
  483.0 2.1 bitcast_dynamic-update-slice_fusion.5
  486.9 3.2 multiply_convert_fusion.3
  490.0 3.2 fusion.126
  493.3 1.8 bitcast_dynamic-update-slice_fusion.4
  495.1 2.1 bitcast_dynamic-update-slice_fusion.5
  499.0 3.2 multiply_convert_fusion.3
  502.1 3.2 fusion.126
  505.3 1.8 bitcast_dynamic-update-slice_fusion.4
  507.1 2.1 bitcast_dynamic-update-slice_fusion.5
  511.0 3.2 multiply_convert_fusion.3
  514.1 3.2 fusion.126
  519.1 2.1 bitcast_dynamic-update-slice_fusion.5
  521.3 11.9 %copy.115 = bf16[8,768,5,128]{3,2,1,0:T(8,128)(2,1)} copy(bf16[8,768,5,128]{3,1,2,0:T(8,128)(2,1)} %get-tuple-element.108) | data formatting | bytes 15728640
  533.2 9.6 copy.124
  542.9 12.0 %copy.116 = bf16[8,768,5,128]{3,2,1,0:T(8,128)(2,1)} copy(bf16[8,768,5,128]{3,1,2,0:T(8,128)(2,1)} %get-tuple-element.109) | data formatting | bytes 15728640
  554.9 9.8 copy.123
  568.8 104.0 %all-reduce.5.cloned.1.call-done = (bf16[512,640]{0,1:T(8,128)(2,1)}, bf16[512,640]{1,0:T(8,128)(2,1)}) async-done(((bf16[512,640]{0,1:T(8,128)(2,1)}, bf16[512,640]{1,0:T(8,128)(2,1)}), (bf16[512,640]{0,1:T(8,128)(2,1)}, bf16[512,640]{1,0:T(8,128)(2,1)})) %all-reduce.5.cloned.1.call-update) | async-done | bytes 1310736 | tf_op jit(solution)/shard_map/psum | solution.py:180
  674.6 179.2 %reduce-scatter.7.cloned.1.call-done = bf16[192,640]{1,0:T(8,128)(2,1)} async-done(((bf16[6144,640]{1,0:T(8,128)(2,1)}), bf16[192,640]{1,0:T(8,128)(2,1)}) %reduce-scatter.7.cloned.1.call-update) | async-done | bytes 245776 | tf_op jit(solution)/shard_map/reduce_scatter | solution.py:155
  854.9 7.3 all-reduce
  867.7 163.5 %reduce-scatter.9.cloned.1.call-done = bf16[192,640]{1,0:T(8,128)(2,1)} async-done(((bf16[6144,640]{1,0:T(8,128)(2,1)}), bf16[192,640]{1,0:T(8,128)(2,1)}) %reduce-scatter.9.cloned.1.call-update) | async-done | bytes 245776
  (166 shorter events, 55.3 us)
Async XLA Ops:
  7.2 12.9 %copy-start.12 = (bf16[192,640]{1,0:T(8,128)(2,1)S(1)}, bf16[192,640]{1,0:T(8,128)(2,1)}, u32[]{:S(2)}) copy-start(bf16[192,640]{1,0:T(8,128)(2,1)} %param.17) | copy-start | bytes 737284
  7.2 12.9 %copy-start.23 = (f32[640]{0:T(1024)S(1)}, f32[640]{0:T(1024)}, u32[]{:S(2)}) copy-start(f32[640]{0:T(1024)} %param.25) | copy-start | bytes 7684
  7.2 14.6 %copy-start.18 = (bf16[192,640]{1,0:T(8,128)(2,1)S(1)}, bf16[192,640]{1,0:T(8,128)(2,1)}, u32[]{:S(2)}) copy-start(bf16[192,640]{1,0:T(8,128)(2,1)} %param.21) | copy-start | bytes 737284
  7.2 14.7 %copy-start.16 = (bf16[512,640]{1,0:T(8,128)(2,1)S(1)}, bf16[512,640]{1,0:T(8,128)(2,1)}, u32[]{:S(2)}) copy-start(bf16[512,640]{1,0:T(8,128)(2,1)} %param.23) | copy-start | bytes 1966084
  7.2 183.1 %all-gather.3.cloned.1.call-start = ((), (), s32[]{:S(2)}) async-start(), calls=%async_computation.2 | async-start | bytes 8110080 | tf_op jit(solution)/shard_map/all_gather | solution.py:145
  8.5 26.5 %copy-start.8 = (bf16[192,640]{0,1:T(8,128)(2,1)}, bf16[192,640]{0,1:T(8,128)(2,1)S(1)}, u32[]{:S(2)}) copy-start(bf16[192,640]{0,1:T(8,128)(2,1)S(1)} %copy.67) | copy-start | bytes 737284
  9.7 13.4 %copy-start.21 = (f32[640]{0:T(1024)S(1)}, f32[640]{0:T(1024)}, u32[]{:S(2)}) copy-start(f32[640]{0:T(1024)} %param.26) | copy-start | bytes 7684
  10.8 12.4 %copy-start.6 = (bf16[192,640]{0,1:T(8,128)(2,1)}, bf16[192,640]{0,1:T(8,128)(2,1)S(1)}, u32[]{:S(2)}) copy-start(bf16[192,640]{0,1:T(8,128)(2,1)S(1)} %copy.83) | copy-start | bytes 737284
  10.9 12.4 %copy-start.22 = (f32[640]{0:T(1024)S(1)}, f32[640]{0:T(1024)}, u32[]{:S(2)}) copy-start(f32[640]{0:T(1024)} %param.27) | copy-start | bytes 7684
  12.3 11.1 %copy-start.2 = (bf16[512,640]{0,1:T(8,128)(2,1)}, bf16[512,640]{0,1:T(8,128)(2,1)S(1)}, u32[]{:S(2)}) copy-start(bf16[512,640]{0,1:T(8,128)(2,1)S(1)} %copy.84) | copy-start | bytes 1966084
  20.9 337.7 %all-gather.5.cloned.1.call-start = ((), (), s32[]{:S(2)}) async-start(), calls=%async_computation.3 | async-start | bytes 8110080 | tf_op jit(solution)/shard_map/all_gather | solution.py:146
  21.7 651.1 %all-reduce.5.cloned.1.call-start = ((), (), s32[]{:S(2)}) async-start(), calls=%async_computation.6 | async-start | bytes 2621440 | tf_op jit(solution)/shard_map/psum | solution.py:180
  23.0 1.8 copy-start.14
  23.4 0.8 copy-start.10
  30.6 4.5 copy-start.20
  32.5 1.0 copy-start.4
  33.5 1.9 copy-start.19
  34.7 819.0 %reduce-scatter.7.cloned.1.call-start = ((), (), s32[]{:S(2)}) async-start(), calls=%async_computation.4 | async-start | bytes 8110080 | tf_op jit(solution)/shard_map/reduce_scatter | solution.py:155
  429.9 3.1 copy-start
  441.8 3.2 copy-start
  453.9 3.2 copy-start
  466.0 3.2 copy-start
  478.0 3.2 copy-start
  490.0 3.2 copy-start
  502.1 3.2 copy-start
  514.1 3.2 copy-start
  542.9 488.3 %reduce-scatter.9.cloned.1.call-start = ((), (), s32[]{:S(2)}) async-start(), calls=%async_computation.5 | async-start | bytes 8110080
  564.7 1.2 copy-start.5
  564.7 1.4 copy-start.11
  566.1 2.5 copy-start.7
  566.1 106.7 %copy-start.3 = (bf16[512,640]{0,1:T(8,128)(2,1)S(1)}, bf16[512,640]{0,1:T(8,128)(2,1)}, u32[]{:S(2)}) copy-start(bf16[512,640]{0,1:T(8,128)(2,1)} %copy-done.2) | copy-start | bytes 1966084
  566.1 108.1 %copy-start.1 = (f32[192,5,128]{2,0,1:T(8,128)S(1)}, f32[192,5,128]{2,0,1:T(8,128)}, u32[]{:S(2)}) copy-start(f32[192,5,128]{2,0,1:T(8,128)} %get-tuple-element.107) | copy-start | bytes 1474564
  566.1 108.3 %copy-start.9 = (bf16[192,640]{0,1:T(8,128)(2,1)S(1)}, bf16[192,640]{0,1:T(8,128)(2,1)}, u32[]{:S(2)}) copy-start(bf16[192,640]{0,1:T(8,128)(2,1)} %copy-done.8) | copy-start | bytes 737284
  567.3 286.5 %copy-start.13 = (bf16[192,640]{1,0:T(8,128)(2,1)S(1)}, bf16[192,640]{1,0:T(8,128)(2,1)}, u32[]{:S(2)}) copy-start(bf16[192,640]{1,0:T(8,128)(2,1)} %param.17) | copy-start | bytes 737284
  862.3 4.4 copy-start.15
  863.2 168.0 %copy-start.17 = (bf16[512,640]{1,0:T(8,128)(2,1)S(1)}, bf16[512,640]{1,0:T(8,128)(2,1)}, u32[]{:S(2)}) copy-start(bf16[512,640]{1,0:T(8,128)(2,1)} %get-tuple-element.486) | copy-start | bytes 1966084
Sparse Core Ops, SparseCore 0:
  21.1 169.2 all-gather.2
  192.0 166.6 all-gather.4
  361.7 310.9 all-reduce.4
  675.2 178.5 reduce-scatter.6
  856.6 174.5 reduce-scatter.8
where the time goes:
time: 1040 us
  waiting for transfers between devices  742 us (71%)
  matrix products  134 us (13%)
  local copies, waits for them, and re-layouts  116 us (11%)
  other arithmetic  16.5 us (2%)
  blocking collectives  14.6 us (1%)
  between operations  14.2 us (1%)
    reduce_scatter x1, waiting for transfers between devices, local(): lax.psum_scatter(stacked[0].reshape(key_all.shape).astype(jnp.bfloat16),...  179 us
    unnamed x6, waiting for transfers between devices  164 us
    all_gather x1, waiting for transfers between devices, local(): lax.all_gather(key_norm, 'ctx', axis=0, tiled=True)  155 us
    all_gather x1, waiting for transfers between devices, local(): lax.all_gather(v_self, 'ctx', axis=0, tiled=True)  140 us
    psum x1, waiting for transfers between devices, local(): lax.psum(cross_terms[1].reshape(text_rows, -1).astype(jnp.bfloat16), 'ctx')  104 us
    unnamed x64, local copies, waits for them, and re-layouts  75.8 us
    reshape x2, local copies, waits for them, and re-layouts, into_blocks(): return tensor.reshape(tensor.shape[0] // span, span, -1, HD)  36.2 us
    dot_general x9, matrix products, backward_terms(): jnp.einsum('qhd,khd->hqk', grad_heads, value_heads, preferred_element_typ...  27.4 us
  transfers between devices with their start and end apart: 5, of which 5 were waited for; matrix products, arithmetic and copies ran while one was open for 25% of the time, Pallas kernels for 0%

commit v1 on v0

--- a/solution.py
+++ b/solution.py
@@ -5,6 +5,11 @@
 
 HD = 128
 epsilon = 1e-06
+
+
+def tell_words(t0):
+    u1 = jax.lax.all_gather(t0, "ctx").sum(axis=0)
+    return u1
 
 
 def squares(tensor):
@@ -177,9 +182,7 @@
         cross_heads, cross_grads, cross_logsum, cross_deltas, text_heads, text_values
     )
     text_key_grad, text_value_grad = (
-        lax.psum(cross_terms[1].reshape(text_rows, -1).astype(jnp.bfloat16), "ctx").astype(
-            jnp.float32
-        ),
+        tell_words(cross_terms[1].reshape(text_rows, -1).astype(jnp.bfloat16)).astype(jnp.float32),
         lax.psum(cross_terms[2].reshape(text_rows, -1).astype(jnp.bfloat16), "ctx").astype(
             jnp.float32
         ),

time: 1040 us -> 1450 us (1.39)
  waiting for transfers between devices: 742 us -> 1130 us
    all_gather x0 -> x1, waiting for transfers between devices: none -> 231 us  [tell_words(): u1 = jax.lax.all_gather(t0, 'ctx').sum(axis=0)]
    psum x1, waiting for transfers between devices: 104 us -> 273 us  [local(): lax.psum(cross_terms[2].reshape(text_rows, -1).astype(jnp.bfloat16), 'ctx')]
    reduce_scatter x1, waiting for transfers between devices: 179 us -> 135 us  [local(): lax.psum_scatter(stacked[0].reshape(key_all.shape).astype(jnp.bfloat16),...]
    unnamed x6 -> x7, waiting for transfers between devices: 164 us -> 181 us
    unnamed x64 -> x50, local copies, waits for them, and re-layouts: 75.8 us -> 74.3 us
  transfers between devices with their start and end apart: 5 -> 6, of which waited for: 5 -> 6; matrix products, arithmetic and copies ran while one was open for 25% -> 6% of each run, Pallas kernels for 0% -> 0%
where the time goes in v1:
time: 1450 us; the launch traced here: 1440 us
  waiting for transfers between devices  1130 us (78%)
  matrix products  135 us (9%)
  local copies, waits for them, and re-layouts  118 us (8%)
  other arithmetic  30.1 us (2%)
  blocking collectives  15.3 us (1%)
  between operations  14.5 us (1%)
    psum x1, waiting for transfers between devices, local(): lax.psum(cross_terms[2].reshape(text_rows, -1).astype(jnp.bfloat16), 'ctx')  273 us
    all_gather x1, waiting for transfers between devices, tell_words(): u1 = jax.lax.all_gather(t0, 'ctx').sum(axis=0)  231 us
    unnamed x7, waiting for transfers between devices  181 us
    all_gather x1, waiting for transfers between devices, local(): lax.all_gather(key_norm, 'ctx', axis=0, tiled=True)  168 us
    all_gather x1, waiting for transfers between devices, local(): lax.all_gather(v_self, 'ctx', axis=0, tiled=True)  140 us
    reduce_scatter x1, waiting for transfers between devices, local(): lax.psum_scatter(stacked[0].reshape(key_all.shape).astype(jnp.bfloat16),...  135 us
    unnamed x50, local copies, waits for them, and re-layouts  74.3 us
    reshape x2, local copies, waits for them, and re-layouts, into_blocks(): return tensor.reshape(tensor.shape[0] // span, span, -1, HD)  36.2 us
  transfers between devices with their start and end apart: 6, of which 6 were waited for; matrix products, arithmetic and copies ran while one was open for 6% of the time, Pallas kernels for 0%

profile of v1, /device:TPU:4, one launch (start us, length us, event | category | flops | bytes accessed | tf_op | source)
XLA Modules:
  0.0 1441.8 jit_solution(8070574441974994948)
XLA Ops:
  12.3 7.4 all-reduce.1
  23.2 167.7 %all-gather.4.cloned.1.call-done = bf16[6144,640]{1,0:T(8,128)(2,1)} async-done(((bf16[192,640]{1,0:T(8,128)(2,1)}), bf16[6144,640]{1,0:T(8,128)(2,1)}) %all-gather.4.cloned.1.call-update) | async-done | bytes 7864336 | tf_op jit(solution)/shard_map/all_gather | solution.py:150
  190.9 18.1 %reshape.110 = bf16[8,768,5,128]{3,2,1,0:T(8,128)(2,1)} reshape(bf16[6144,640]{1,0:T(8,128)(2,1)} %all-gather.4.cloned.1.call-done) | data formatting | bytes 15728640 | tf_op jit(solution)/shard_map/reshape | solution.py:30
  209.0 9.9 copy.108
  218.9 140.3 %all-gather.6.cloned.1.call-done = bf16[6144,640]{1,0:T(8,128)(2,1)} async-done(((bf16[192,640]{1,0:T(8,128)(2,1)}), bf16[6144,640]{1,0:T(8,128)(2,1)}) %all-gather.6.cloned.1.call-update) | async-done | bytes 7864336 | tf_op jit(solution)/shard_map/all_gather | solution.py:151
  359.2 18.1 %reshape.111 = bf16[8,768,5,128]{3,2,1,0:T(8,128)(2,1)} reshape(bf16[6144,640]{1,0:T(8,128)(2,1)} %all-gather.6.cloned.1.call-done) | data formatting | bytes 15728640 | tf_op jit(solution)/shard_map/reshape | solution.py:30
  377.3 10.0 copy.106
  387.3 38.2 %while.30 = (s32[]{:T(128)}, f32[5,192]{1,0:T(8,128)S(1)}, f32[5,192]{1,0:T(8,128)S(1)}, f32[5,192]{1,0:T(8,128)S(1)}, bf16[8,768,5,128]{3,1,2,0:T(8,128)(2,1)},...) while((s32[]{:T(128)}, f32[5,192]{1,0:T(8,128)S(1)}, ...), condition=%wide.region_8.9_spmd.clone, body=%wide.region_4.8_spmd.clone.sunk | while | flops 384129600 | bytes 11374208 | solution.py:100
  389.1 2.1 fusion.112
  392.0 1.8 bitcast_reduce_fusion.2
  393.9 2.1 fusion.112
  396.8 1.8 bitcast_reduce_fusion.2
  398.7 2.1 fusion.112
  401.6 1.8 bitcast_reduce_fusion.2
  403.5 2.1 fusion.112
  406.4 1.8 bitcast_reduce_fusion.2
  408.2 2.1 fusion.112
  411.1 1.8 bitcast_reduce_fusion.2
  413.0 2.1 fusion.112
  415.9 1.8 bitcast_reduce_fusion.2
  417.8 2.1 fusion.112
  420.7 1.8 bitcast_reduce_fusion.2
  422.6 2.1 fusion.112
  425.5 96.2 %while.31 = (s32[]{:T(128)}, f32[192,5,128]{2,0,1:T(8,128)}, bf16[8,768,5,128]{3,1,2,0:T(8,128)(2,1)}, bf16[8,768,5,128]{3,1,2,0:T(8,128)(2,1)}, bf16[8,768,5,12...) while((s32[]{:T(128)}, f32[192,5,128]{2,0,1:T(8,128)}, ...), condition=%wide.region_10.0_spmd.clone, body=%wide.region_9.0_spmd.clone.sunk | while | flops 950476800 | bytes 28028344 | solution.py:109
  427.2 3.2 multiply_convert_fusion.3
  430.4 3.1 fusion.126
  435.3 2.2 bitcast_dynamic-update-slice_fusion.5
  439.2 3.2 multiply_convert_fusion.3
  442.4 3.2 fusion.126
  445.6 1.9 bitcast_dynamic-update-slice_fusion.4
  447.4 2.1 bitcast_dynamic-update-slice_fusion.5
  451.3 3.2 multiply_convert_fusion.3
  454.4 3.2 fusion.126
  459.4 2.1 bitcast_dynamic-update-slice_fusion.5
  463.3 3.2 multiply_convert_fusion.3
  466.5 3.2 fusion.126
  471.5 2.1 bitcast_dynamic-update-slice_fusion.5
  475.3 3.2 multiply_convert_fusion.3
  478.5 3.2 fusion.126
  483.5 2.1 bitcast_dynamic-update-slice_fusion.5
  487.3 3.2 multiply_convert_fusion.3
  490.5 3.2 fusion.126
  493.7 1.8 bitcast_dynamic-update-slice_fusion.4
  495.6 2.1 bitcast_dynamic-update-slice_fusion.5
  499.4 3.2 multiply_convert_fusion.3
  502.5 3.2 fusion.126
  507.6 2.1 bitcast_dynamic-update-slice_fusion.5
  511.4 3.2 multiply_convert_fusion.3
  514.6 3.2 fusion.126
  519.6 2.1 bitcast_dynamic-update-slice_fusion.5
  521.7 11.9 copy.148
  533.6 9.6 copy.157
  552.4 2.2 copy.127
  556.1 2.2 copy.129
  558.3 12.0 copy.149
  570.3 9.8 copy.156
  581.4 2.4 fusion.41
  587.5 135.0 %reduce-scatter.7.cloned.1.call-done = bf16[192,640]{1,0:T(8,128)(2,1)} async-done(((bf16[6144,640]{1,0:T(8,128)(2,1)}), bf16[192,640]{1,0:T(8,128)(2,1)}) %reduce-scatter.7.cloned.1.call-update) | async-done | bytes 245776 | tf_op jit(solution)/shard_map/reduce_scatter | solution.py:160
  723.8 230.7 %all-gather.8.cloned.1.call-done = bf16[32,512,640]{2,1,0:T(8,128)(2,1)} async-done(((bf16[1,512,640]{2,1,0:T(8,128)(2,1)}), bf16[32,512,640]{2,1,0:T(8,128)(2,1)}) %all-gather.8.cloned.1.call-update) | async-done | bytes 20971536 | tf_op jit(solution)/shard_map/all_gather | solution.py:11
  954.5 11.0 reduce_sum.129
  965.9 7.9 all-reduce
  980.0 272.5 %all-reduce.4.cloned.1.call-done = bf16[512,640]{1,0:T(8,128)(2,1)} async-done(((bf16[512,640]{1,0:T(8,128)(2,1)}), bf16[512,640]{1,0:T(8,128)(2,1)}) %all-reduce.4.cloned.1.call-update) | async-done | bytes 655376 | tf_op jit(solution)/shard_map/psum | solution.py:186
  1252.6 180.4 %reduce-scatter.9.cloned.1.call-done = bf16[192,640]{1,0:T(8,128)(2,1)} async-done(((bf16[6144,640]{1,0:T(8,128)(2,1)}), bf16[192,640]{1,0:T(8,128)(2,1)}) %reduce-scatter.9.cloned.1.call-update) | async-done | bytes 245776
  1433.0 2.0 copy.185
  (158 shorter events, 64.5 us)
Async XLA Ops:
  7.2 15.2 %copy-start.14 = (f32[640]{0:T(1024)S(1)}, f32[640]{0:T(1024)}, u32[]{:S(2)}) copy-start(f32[640]{0:T(1024)} %param.24) | copy-start | bytes 7684
  7.2 15.6 %copy-start.12 = (bf16[192,640]{1,0:T(8,128)(2,1)S(1)}, bf16[192,640]{1,0:T(8,128)(2,1)}, u32[]{:S(2)}) copy-start(bf16[192,640]{1,0:T(8,128)(2,1)} %param.19) | copy-start | bytes 737284
  7.2 183.7 %all-gather.4.cloned.1.call-start = ((), (), s32[]{:S(2)}) async-start(), calls=%async_computation.2 | async-start | bytes 8110080 | tf_op jit(solution)/shard_map/all_gather | solution.py:150
  8.4 200.6 %copy-start.7 = (bf16[192,640]{0,1:T(8,128)(2,1)}, bf16[192,640]{0,1:T(8,128)(2,1)S(1)}, u32[]{:S(2)}) copy-start(bf16[192,640]{0,1:T(8,128)(2,1)S(1)} %copy.100) | copy-start | bytes 737284
  10.7 11.8 copy-start.5
  21.5 337.7 %all-gather.6.cloned.1.call-start = ((), (), s32[]{:S(2)}) async-start(), calls=%async_computation.3 | async-start | bytes 8110080 | tf_op jit(solution)/shard_map/all_gather | solution.py:151
  22.3 700.3 %reduce-scatter.7.cloned.1.call-start = ((), (), s32[]{:S(2)}) async-start(), calls=%async_computation.6 | async-start | bytes 8110080 | tf_op jit(solution)/shard_map/reduce_scatter | solution.py:160
  430.4 3.1 copy-start
  442.4 3.2 copy-start
  454.4 3.2 copy-start
  466.5 3.2 copy-start
  478.5 3.2 copy-start
  490.5 3.2 copy-start
  502.5 3.2 copy-start
  514.6 3.2 copy-start
  543.3 1.1 copy-start.2
  543.3 1.1 copy-start.17
  543.3 2.4 copy-start.13
  543.3 2.6 copy-start.11
  543.3 3.7 copy-start.6
  543.3 3.7 copy-start.15
  543.3 411.1 %all-gather.8.cloned.1.call-start = ((), (), s32[]{:S(2)}) async-start(), calls=%async_computation.4 | async-start | bytes 21626880 | tf_op jit(solution)/shard_map/all_gather | solution.py:11
  547.0 1.9 copy-start.10
  550.2 1.0 copy-start.3
  554.6 698.0 %all-reduce.4.cloned.1.call-start = ((), (), s32[]{:S(2)}) async-start(), calls=%async_computation.5 | async-start | bytes 1310720 | tf_op jit(solution)/shard_map/psum | solution.py:186
  558.3 874.7 %reduce-scatter.9.cloned.1.call-start = ((), (), s32[]{:S(2)}) async-start(), calls=%async_computation.7 | async-start | bytes 8110080
  580.2 1.2 copy-start.4
  581.4 3.8 copy-start.1
  581.4 4.9 copy-start.8
  581.4 141.2 %copy-start.9 = (bf16[192,640]{1,0:T(8,128)(2,1)S(1)}, bf16[192,640]{1,0:T(8,128)(2,1)}, u32[]{:S(2)}) copy-start(bf16[192,640]{1,0:T(8,128)(2,1)} %param.17) | copy-start | bytes 737284
  581.4 141.2 %copy-start.16 = (f32[640]{0:T(1024)S(1)}, f32[640]{0:T(1024)}, u32[]{:S(2)}) copy-start(f32[640]{0:T(1024)} %param.25) | copy-start | bytes 7684
Sparse Core Ops, SparseCore 0:
  21.6 169.2 all-gather.3
  192.6 166.6 all-gather.5
  543.4 179.1 reduce-scatter.6
  724.2 230.2 all-gather.7
  957.0 295.5 all-reduce.3
  1255.4 177.4 reduce-scatter.8
